TPU v7x, 32 devices: a whole 2x2x4 slice. The times are simulated.
32 devices in a mesh: ctx: 16 (over z, y, core), head: 2 (over x).
Axes of the slice: x: 2, y: 2, z: 4, core: 2. Of those that a mesh axis runs over, the one named last changes fastest.
Arguments:
- tokens: bfloat16 [8192, 3840], P('ctx', 'head'), may hold values from -18 to 18
- w_query: bfloat16 [3840, 4096], P('ctx', 'head'), may hold values from -0.09375 to 0.09375
- key_matrix: bfloat16 [3840, 2048], P('ctx', 'head'), may hold values from -0.09375 to 0.09375
- value_matrix: bfloat16 [3840, 2048], P('ctx', 'head'), may hold values from -0.09375 to 0.09375
- d_attended: bfloat16 [8192, 4096], P('ctx', 'head'), may hold values from -6 to 6
- doc_lengths: int32 [8], replicated, may hold values from 1 to 2048, 8192 in all
Outputs:
- attended: bfloat16 [8192, 4096], P('ctx', 'head')
- key_grad: bfloat16 [8192, 2048], P('ctx', 'head')
Inputs may be any that keep to these rules, and one draw needn't show every extreme that they name: `doc_lengths`: the documents lie end to end from position 0 and fill all 8192 positions.
All inputs are finite; a program needn't handle non-finite values.
Results may differ from a plain program's by a relative error of at most 0.012.
The roundings to bfloat16 on the way count: a program that leaves them out, or rounds other values in their place, can miss the bound.
Values may be sent and summed in bfloat16 or wider, within the bound.
A program may use at most 128 MiB of HBM per device.

v0:
```python
import functools

import jax
import jax.numpy as jnp
from jax import lax
from jax.experimental import pallas as pl
from jax.experimental.pallas import tpu as pltpu
from jax.sharding import PartitionSpec as P

HEAD_SIZE = 256
WINDOW = 1024
TILE = 128


def shifted(block, axis, distance):
    devices = range(lax.axis_size(axis))
    route = [(i - distance, i) for i in devices if i - distance in devices]
    return lax.ppermute(block, axis, route)


def attend_kernel(count, group, *refs):
    lead_ref, lengths_ref, query_ref, grad_ref = refs[:4]
    key_refs = refs[4 : 4 + count]
    value_refs = refs[4 + count : 4 + 2 * count]
    out_ref = refs[4 + 2 * count]
    sum_refs = refs[5 + 2 * count : 5 + 3 * count]
    keys, values, sums = refs[5 + 3 * count :]
    rows = query_ref.shape[0]
    docs = lengths_ref.shape[0]
    for n in range(count):
        keys[n * rows : (n + 1) * rows] = key_refs[n][...]
        values[n * rows : (n + 1) * rows] = value_refs[n][...]
    sums[...] = jnp.zeros_like(sums)
    lead = lead_ref[0]
    span = WINDOW + TILE

    def one_tile(t, carry):
        first = pl.multiple_of(t * TILE, TILE)
        window = pl.ds(first, span)
        row_pos = lead + first + lax.broadcasted_iota(jnp.int32, (TILE, 1), 0)
        key_pos = lead + first - WINDOW + lax.broadcasted_iota(jnp.int32, (1, span), 1)
        begin = jnp.zeros_like(row_pos)
        start = jnp.int32(0)
        for d in range(docs):
            begin = jnp.where(row_pos >= start, start, begin)
            start = start + lengths_ref[d]
        least = jnp.maximum(begin, row_pos - (WINDOW - 1))
        allowed = (key_pos >= least) & (key_pos <= row_pos)
        key = keys[window, :]
        value = values[window, :]
        total = sums[window, :]
        for e in range(group):
            columns = slice(e * HEAD_SIZE, (e + 1) * HEAD_SIZE)
            query = query_ref[pl.ds(first, TILE), columns]
            grad = grad_ref[pl.ds(first, TILE), columns]
            scores = lax.dot_general(
                query, key, (((1,), (1,)), ((), ())), preferred_element_type=jnp.float32
            )
            dprob = lax.dot_general(
                grad, value, (((1,), (1,)), ((), ())), preferred_element_type=jnp.float32
            )
            scores = jnp.where(allowed, scores, -1e30)
            expo = jnp.exp(scores - jnp.max(scores, axis=1, keepdims=True))
            probs = expo * (1.0 / jnp.sum(expo, axis=1, keepdims=True))
            out = jnp.dot(probs.astype(jnp.bfloat16), value, preferred_element_type=jnp.float32)
            out_ref[pl.ds(first, TILE), columns] = out.astype(jnp.bfloat16)
            delta = jnp.sum(probs * dprob, axis=1, keepdims=True)
            dscore = (probs * (dprob - delta)).astype(jnp.bfloat16)
            total = total + lax.dot_general(
                dscore, query, (((0,), (0,)), ((), ())), preferred_element_type=jnp.float32
            )
        sums[window, :] = total
        return carry

    lax.fori_loop(0, rows // TILE, one_tile, 0)
    for n in range(count):
        sum_refs[n][...] = sums[n * rows : (n + 1) * rows].astype(sum_refs[n].dtype)


def attend(query, grad_rows, joined, lead, lengths, first_head, heads):
    rows = query.shape[0]
    count = len(joined)
    kv_heads = joined[0].shape[1] // (2 * HEAD_SIZE)
    group = query.shape[1] // (kv_heads * HEAD_SIZE)
    wide = pl.BlockSpec((rows, group * HEAD_SIZE), lambda g: (0, first_head + g))
    key_spec = pl.BlockSpec((rows, HEAD_SIZE), lambda g: (0, first_head + g))
    value_spec = pl.BlockSpec((rows, HEAD_SIZE), lambda g: (0, kv_heads + first_head + g))
    sum_spec = pl.BlockSpec((rows, HEAD_SIZE), lambda g: (0, g))
    scalars = pl.BlockSpec(memory_space=pltpu.SMEM)
    kinds = [jnp.bfloat16] * (count - 1) + [jnp.float32]
    outs = pl.pallas_call(
        functools.partial(attend_kernel, count, group),
        grid=(heads,),
        in_specs=[scalars, scalars, wide, wide] + [key_spec] * count + [value_spec] * count,
        out_specs=[pl.BlockSpec((rows, group * HEAD_SIZE), lambda g: (0, g))] + [sum_spec] * count,
        out_shape=[jax.ShapeDtypeStruct((rows, heads * group * HEAD_SIZE), jnp.bfloat16)]
        + [jax.ShapeDtypeStruct((rows, heads * HEAD_SIZE), kind) for kind in kinds],
        scratch_shapes=[
            pltpu.VMEM((count * rows, HEAD_SIZE), jnp.bfloat16),
            pltpu.VMEM((count * rows, HEAD_SIZE), jnp.bfloat16),
            pltpu.VMEM((count * rows, HEAD_SIZE), jnp.float32),
        ],
        compiler_params=pltpu.CompilerParams(vmem_limit_bytes=40 * 2**20),
        cost_estimate=pl.CostEstimate(
            flops=10 * heads * group * rows * (WINDOW + TILE) * HEAD_SIZE,
            bytes_accessed=heads * rows * HEAD_SIZE * 2 * (3 * group + 5 * count),
            transcendentals=heads * group * rows * (WINDOW + TILE),
        ),
    )(lead, lengths, query, grad_rows, *joined, *joined)
    return outs[0], outs[1:]


def local(tokens, w_query, key_matrix, value_matrix, d_attended, doc_lengths):
    features = lax.all_gather(tokens, "head", axis=1, tiled=True)
    rows_here = features.shape[0]
    kv_heads = key_matrix.shape[1] // HEAD_SIZE

    def project(piece):
        whole = lax.all_gather(piece, "ctx", axis=0, tiled=True)
        return jnp.dot(features, whole, preferred_element_type=jnp.float32)

    query = (project(w_query) * 0.0625).astype(jnp.bfloat16)
    keys = project(key_matrix).astype(jnp.bfloat16)
    values = project(value_matrix).astype(jnp.bfloat16)
    blocks = WINDOW // rows_here
    joined = [jnp.concatenate([keys, values], axis=1)]
    for _ in range(blocks):
        joined = [shifted(joined[0], "ctx", 1)] + joined
    lead = (lax.axis_index("ctx") * rows_here).astype(jnp.int32).reshape(1)
    attended, shares = attend(query, d_attended, joined, lead, doc_lengths, 0, kv_heads)
    total = shares[0]
    for share in shares[1:-1]:
        moved = shifted(total, "ctx", -1).astype(jnp.float32)
        total = (moved + share.astype(jnp.float32)).astype(jnp.bfloat16)
    key_grad = shifted(total, "ctx", -1).astype(jnp.float32) + shares[-1]
    return (attended, key_grad.astype(jnp.bfloat16))


def solution(mesh):
    return jax.shard_map(
        local,
        mesh=mesh,
        in_specs=(
            P("ctx", "head"),
            P("ctx", "head"),
            P("ctx", "head"),
            P("ctx", "head"),
            P("ctx", "head"),
            P(),
        ),
        out_specs=(P("ctx", "head"), P("ctx", "head")),
        check_vma=False,
    )
```

profile of v0, /device:TPU:13, one launch (start us, length us, event | category | flops | bytes accessed | tf_op | source)
XLA Modules:
  0.0 457.6 jit_solution(4890918764317005016)
XLA Ops:
  7.2 0.0 all-gather.5.cloned.1.call-start
  7.2 0.7 all-gather.5.cloned.1.call-update
  7.9 0.0 all-gather.9.cloned.1.call-start
  7.9 0.7 all-gather.9.cloned.1.call-update
  8.6 0.0 all-gather.11.cloned.1.call-start
  8.7 0.7 all-gather.11.cloned.1.call-update
  9.4 0.0 all-gather.7.cloned.1.call-start
  9.4 0.5 all-gather.7.cloned.1.call-update
  10.0 54.5 %all-gather.5.cloned.1.call-done = bf16[512,3840]{1,0:T(8,128)(2,1)} async-done(((bf16[512,1920]{1,0:T(8,128)(2,1)}), bf16[512,3840]{1,0:T(8,128)(2,1)}) %all-gather.5.cloned.1.call-update) | async-done | bytes 3932176 | tf_op jit(solution)/shard_map/all_gather | solution.py:114
  64.5 73.0 %all-gather.9.cloned.1.call-done = bf16[3840,1024]{1,0:T(8,128)(2,1)} async-done(((bf16[240,1024]{1,0:T(8,128)(2,1)}), bf16[3840,1024]{1,0:T(8,128)(2,1)}) %all-gather.9.cloned.1.call-update) | async-done | bytes 7864336 | tf_op jit(solution)/shard_map/all_gather | solution.py:119
  137.5 8.6 %convolution_convert_fusion.1 = bf16[512,1024]{1,0:T(8,128)(2,1)S(1)} fusion(bf16[512,3840]{1,0:T(8,128)(2,1)} %all-gather.5.cloned.1.call-done, bf16[3840,1024]{1,0:T(8,128)(2,1)} %all-gather.9.cloned.1.call-done), kind=kOutput, calls=%fused_computation.5 | convolution fusion | flops 4027056128 | bytes 12845056 | tf_op jit(solution)/shard_map/dot_general | solution.py:120
  146.1 63.6 %all-gather.11.cloned.1.call-done = bf16[3840,1024]{1,0:T(8,128)(2,1)} async-done(((bf16[240,1024]{1,0:T(8,128)(2,1)}), bf16[3840,1024]{1,0:T(8,128)(2,1)}) %all-gather.11.cloned.1.call-update) | async-done | bytes 7864336 | tf_op jit(solution)/shard_map/all_gather | solution.py:119
  209.7 8.6 %convolution_convert_fusion = bf16[512,1024]{1,0:T(8,128)(2,1)S(1)} fusion(bf16[512,3840]{1,0:T(8,128)(2,1)} %all-gather.5.cloned.1.call-done, bf16[3840,1024]{1,0:T(8,128)(2,1)} %all-gather.11.cloned.1.call-done), kind=kOutput, calls=%fused_computation.4 | convolution fusion | flops 4027056128 | bytes 12845056 | tf_op jit(solution)/shard_map/dot_general | solution.py:120
  218.4 0.2 pad_maximum_fusion.refs_6_.refs_9_
  218.6 0.0 copy-start.2
  218.6 1.4 copy-done.2
  219.9 3.8 collective-permute-start
  223.8 61.1 %collective-permute-done.refs_5_.refs_8_ = bf16[512,2048]{1,0:T(8,128)(2,1)} collective-permute-done((bf16[512,2048]{1,0:T(8,128)(2,1)S(1)}, bf16[512,2048]{1,0:T(8,128)(2,1)}, u32[]{:S(2)}, u32[]{:S(2)}) %collective-permute-start) | collective-permute-done | bytes 2097184 | tf_op jit(solution)/shard_map/ppermute | solution.py:18
  284.9 5.4 %collective-permute-start.1 = (bf16[512,2048]{1,0:T(8,128)(2,1)}, bf16[512,2048]{1,0:T(8,128)(2,1)}, u32[]{:S(2)}, u32[]{:S(2)}) collective-permute-start(bf16[512,2048]{1,0:T(8,128)(2,1)} %collective-permute-done.refs_5_.refs_8_), channel_id=1, source_target_pairs={{0,2},{2,4},{4,6},{6,8},{8,10},{10,12},{12,14},{14,16},{16,18},{18... | collective-permute-start | bytes 6291464 | tf_op jit(solution)/shard_map/ppermute | solution.py:18
  290.3 0.0 copy-start
  290.3 0.0 copy-start.1
  290.3 74.1 %all-gather.7.cloned.1.call-done = bf16[3840,2048]{1,0:T(8,128)(2,1)} async-done(((bf16[240,2048]{1,0:T(8,128)(2,1)}), bf16[3840,2048]{1,0:T(8,128)(2,1)}) %all-gather.7.cloned.1.call-update) | async-done | bytes 15728656 | tf_op jit(solution)/shard_map/all_gather | solution.py:119
  364.4 12.8 %multiply_convert_fusion.refs_2_ = bf16[512,2048]{1,0:T(8,128)(2,1)S(1)} fusion(bf16[512,3840]{1,0:T(8,128)(2,1)} %all-gather.5.cloned.1.call-done, bf16[3840,2048]{1,0:T(8,128)(2,1)} %all-gather.7.cloned.1.call-done), kind=kOutput, calls=%fused_computation | convolution fusion | flops 8055160832 | bytes 21757952 | tf_op jit(solution)/shard_map/dot_general | solution.py:120
  377.2 0.0 collective-permute-done.1.refs_4_.refs_7_
  377.2 0.0 copy-done
  377.2 0.0 copy-done.1
  377.2 38.0 %shard_map.77 = (bf16[512,2048]{1,0:T(8,128)(2,1)}, bf16[512,1024]{1,0:T(8,128)(2,1)S(1)}, bf16[512,1024]{1,0:T(8,128)(2,1)S(1)}, f32[512,1024]{1,0:T(8,128)S(1)}) custom-call(s32[1]{0:T(128)} %bitcast.refs_0_, s32[8]{0:T(128)S(1)} %copy-done.1, bf16[512,2048]{1,0:T(8,128)(2,1)S(1)} %multiply_convert_fusion.refs_2_, bf16[512,2048]{1,0:T(8,128)(2,1)S(1)} %copy-done, ...), custom_call_target="tpu_custom_call" | custom-call | flops 12079595520 | bytes 22020096 | tf_op jit(solution)/shard_map/pallas_call | solution.py:91
  415.2 2.2 collective-permute-start.2
  417.4 14.8 %collective-permute-done.2 = bf16[512,1024]{1,0:T(8,128)(2,1)S(1)} collective-permute-done((bf16[512,1024]{1,0:T(8,128)(2,1)S(1)}, bf16[512,1024]{1,0:T(8,128)(2,1)S(1)}, u32[]{:S(2)}, u32[]{:S(2)}) %collective-permute-start.2) | collective-permute-done | bytes 1048608 | tf_op jit(solution)/shard_map/ppermute | solution.py:18
  432.3 0.4 add_convert_fusion.1
  432.7 1.9 collective-permute-start.3
  434.6 15.1 %collective-permute-done.3 = bf16[512,1024]{1,0:T(8,128)(2,1)S(1)} collective-permute-done((bf16[512,1024]{1,0:T(8,128)(2,1)S(1)}, bf16[512,1024]{1,0:T(8,128)(2,1)S(1)}, u32[]{:S(2)}, u32[]{:S(2)}) %collective-permute-start.3) | collective-permute-done | bytes 1048608 | tf_op jit(solution)/shard_map/ppermute | solution.py:18
  449.7 1.4 add_convert_fusion
Async XLA Ops:
  7.2 57.3 %all-gather.5.cloned.1.call-start = ((), (), s32[]{:S(2)}) async-start(), calls=%async_computation | async-start | bytes 5898240 | tf_op jit(solution)/shard_map/all_gather | solution.py:114
  7.9 129.6 %all-gather.9.cloned.1.call-start = ((), (), s32[]{:S(2)}) async-start(), calls=%async_computation.2 | async-start | bytes 8355840 | tf_op jit(solution)/shard_map/all_gather | solution.py:119
  8.6 201.1 %all-gather.11.cloned.1.call-start = ((), (), s32[]{:S(2)}) async-start(), calls=%async_computation.3 | async-start | bytes 8355840 | tf_op jit(solution)/shard_map/all_gather | solution.py:119
  9.4 355.0 %all-gather.7.cloned.1.call-start = ((), (), s32[]{:S(2)}) async-start(), calls=%async_computation.1 | async-start | bytes 16711680 | tf_op jit(solution)/shard_map/all_gather | solution.py:119
  218.6 1.4 copy-start.2
  219.9 65.0 %collective-permute-start = (bf16[512,2048]{1,0:T(8,128)(2,1)S(1)}, bf16[512,2048]{1,0:T(8,128)(2,1)}, u32[]{:S(2)}, u32[]{:S(2)}) collective-permute-start(bf16[512,2048]{1,0:T(8,128)(2,1)S(1)} %pad_maximum_fusion.refs_6_.refs_9_), channel_id=1, source_target_pairs={{0,2},{2,4},{4,6},{6,8},{8,10},{10,12},{12,14},{14,16},{16,18},{18... | collective-permute-start | bytes 6291464 | tf_op jit(solution)/shard_map/ppermute | solution.py:18
  284.9 92.3 %collective-permute-start.1 = (bf16[512,2048]{1,0:T(8,128)(2,1)}, bf16[512,2048]{1,0:T(8,128)(2,1)}, u32[]{:S(2)}, u32[]{:S(2)}) collective-permute-start(bf16[512,2048]{1,0:T(8,128)(2,1)} %collective-permute-done.refs_5_.refs_8_), channel_id=1, source_target_pairs={{0,2},{2,4},{4,6},{6,8},{8,10},{10,12},{12,14},{14,16},{16,18},{18... | collective-permute-start | bytes 6291464 | tf_op jit(solution)/shard_map/ppermute | solution.py:18
  290.3 86.9 %copy-start = (bf16[512,2048]{1,0:T(8,128)(2,1)S(1)}, bf16[512,2048]{1,0:T(8,128)(2,1)}, u32[]{:S(2)}) copy-start(bf16[512,2048]{1,0:T(8,128)(2,1)} %refs_3_.1) | copy-start | bytes 6291460
  290.3 86.9 %copy-start.1 = (s32[8]{0:T(128)S(1)}, s32[8]{0:T(128)}, u32[]{:S(2)}) copy-start(s32[8]{0:T(128)} %refs_1_.1) | copy-start | bytes 100
  415.2 17.0 %collective-permute-start.2 = (bf16[512,1024]{1,0:T(8,128)(2,1)S(1)}, bf16[512,1024]{1,0:T(8,128)(2,1)S(1)}, u32[]{:S(2)}, u32[]{:S(2)}) collective-permute-start(bf16[512,1024]{1,0:T(8,128)(2,1)S(1)} %get-tuple-element.7), channel_id=1, source_target_pairs={{2,0},{4,2},{6,4},{8,6},{10,8},{12,10},{14,12},{16,14},{18,16},{20... | collective-permute-start | bytes 3145736 | tf_op jit(solution)/shard_map/ppermute | solution.py:18
  432.7 17.0 %collective-permute-start.3 = (bf16[512,1024]{1,0:T(8,128)(2,1)S(1)}, bf16[512,1024]{1,0:T(8,128)(2,1)S(1)}, u32[]{:S(2)}, u32[]{:S(2)}) collective-permute-start(bf16[512,1024]{1,0:T(8,128)(2,1)S(1)} %add_convert_fusion.1), channel_id=1, source_target_pairs={{2,0},{4,2},{6,4},{8,6},{10,8},{12,10},{14,12},{16,14},{18,16},{20... | collective-permute-start | bytes 3145736 | tf_op jit(solution)/shard_map/ppermute | solution.py:18
Sparse Core Ops, SparseCore 0:
  9.5 54.8 all-gather.4
  66.8 70.6 all-gather.8
  139.8 69.9 all-gather.10
  211.9 152.4 all-gather.6
where the time goes:
time: 458 us
  waiting for transfers between devices  359 us (78%)
  Pallas kernels  38 us (8%)
  matrix products  30.1 us (7%)
  between operations  13.9 us (3%)
  starting transfers between devices  13.4 us (3%)
    all_gather x3, waiting for transfers between devices, project(): whole = lax.all_gather(piece, 'ctx', axis=0, tiled=True)  211 us
    ppermute x4, waiting for transfers between devices, shifted(): return lax.ppermute(block, axis, route)  91.1 us
    all_gather x1, waiting for transfers between devices, local(): features = lax.all_gather(tokens, 'head', axis=1, tiled=True)  54.5 us
    pallas_call x1, Pallas kernels, attend(): pl.pallas_call(functools.partial(attend_kernel, count, group), grid=(head...  38 us
    dot_general x3, matrix products, project(): return jnp.dot(features, whole, preferred_element_type=jnp.float32)  30.1 us
    ppermute x4, starting transfers between devices, shifted(): return lax.ppermute(block, axis, route)  13.3 us
  transfers between devices with their start and end apart: 8, of which 7 were waited for; matrix products, arithmetic and copies ran while one was open for 7% of the time, Pallas kernels for 0%

commit v1 on v0

--- a/solution.py
+++ b/solution.py
@@ -5,6 +5,7 @@
 from jax import lax
 from jax.experimental import pallas as pl
 from jax.experimental.pallas import tpu as pltpu
+from jax.sharding import Mesh
 from jax.sharding import PartitionSpec as P
 
 HEAD_SIZE = 256
@@ -13,7 +14,7 @@
 
 
 def shifted(block, axis, distance):
-    devices = range(lax.axis_size(axis))
+    devices = range(lax.axis_size("chip") * lax.axis_size("core"))
     route = [(i - distance, i) for i in devices if i - distance in devices]
     return lax.ppermute(block, axis, route)
 
@@ -110,44 +111,75 @@
     return outs[0], outs[1:]
 
 
+def from_partner(block):
+    return lax.ppermute(block, "core", [(0, 1), (1, 0)])
+
+
+def in_core_order(own, other):
+    first = lax.axis_index("core") == 0
+    return jnp.where(first, own, other), jnp.where(first, other, own)
+
+
+def gather_features(tokens):
+    count, width = lax.axis_size("head"), tokens.shape[1]
+    me = lax.axis_index("head")
+    features = jnp.zeros((tokens.shape[0], count * width), tokens.dtype)
+    features = lax.dynamic_update_slice(features, tokens, (0, me * width))
+    for step in range(1, count):
+        moved = lax.ppermute(tokens, "head", [(i, (i + step) % count) for i in range(count)])
+        source = lax.rem(me - step + count, count)
+        features = lax.dynamic_update_slice(features, moved, (0, source * width))
+    return features
+
+
+def half_columns(weights):
+    half = weights.shape[1] // 2
+    left, right = weights[:, :half], weights[:, half:]
+    first = lax.axis_index("core") == 0
+    keep, send = jnp.where(first, left, right), jnp.where(first, right, left)
+    return jnp.concatenate(in_core_order(keep, from_partner(send)), axis=0)
+
+
 def local(tokens, w_query, key_matrix, value_matrix, d_attended, doc_lengths):
-    features = lax.all_gather(tokens, "head", axis=1, tiled=True)
-    rows_here = features.shape[0]
+    rows_here = tokens.shape[0]
     kv_heads = key_matrix.shape[1] // HEAD_SIZE
+    features = gather_features(tokens)
+    kv_piece = jnp.concatenate([half_columns(key_matrix), half_columns(value_matrix)], axis=1)
+    kv_whole = lax.all_gather(kv_piece, "chip", axis=0, tiled=True)
+    kv_whole, query_piece = lax.optimization_barrier((kv_whole, half_columns(w_query)))
+    query_whole = lax.all_gather(query_piece, "chip", axis=0, tiled=True)
+    theirs = from_partner(features)
 
-    def project(piece):
-        whole = lax.all_gather(piece, "ctx", axis=0, tiled=True)
-        return jnp.dot(features, whole, preferred_element_type=jnp.float32)
+    def project(whole, factor):
+        mine = jnp.dot(features, whole, preferred_element_type=jnp.float32) * factor
+        others = jnp.dot(theirs, whole, preferred_element_type=jnp.float32) * factor
+        return in_core_order(mine.astype(jnp.bfloat16), from_partner(others.astype(jnp.bfloat16)))
 
-    query = (project(w_query) * 0.0625).astype(jnp.bfloat16)
-    keys = project(key_matrix).astype(jnp.bfloat16)
-    values = project(value_matrix).astype(jnp.bfloat16)
+    left, right = project(kv_whole, 1.0)
+    half = key_matrix.shape[1] // 2
     blocks = WINDOW // rows_here
-    joined = [jnp.concatenate([keys, values], axis=1)]
+    joined = [jnp.concatenate([left[:, :half], right[:, :half], left[:, half:], right[:, half:]], axis=1)]
     for _ in range(blocks):
-        joined = [shifted(joined[0], "ctx", 1)] + joined
-    lead = (lax.axis_index("ctx") * rows_here).astype(jnp.int32).reshape(1)
+        joined = [shifted(joined[0], ("chip", "core"), 1)] + joined
+    query = jnp.concatenate(project(query_whole, 0.0625), axis=1)
+    lead = (lax.axis_index(("chip", "core")) * rows_here).astype(jnp.int32).reshape(1)
     attended, shares = attend(query, d_attended, joined, lead, doc_lengths, 0, kv_heads)
     total = shares[0]
     for share in shares[1:-1]:
-        moved = shifted(total, "ctx", -1).astype(jnp.float32)
+        moved = shifted(total, ("chip", "core"), -1).astype(jnp.float32)
         total = (moved + share.astype(jnp.float32)).astype(jnp.bfloat16)
-    key_grad = shifted(total, "ctx", -1).astype(jnp.float32) + shares[-1]
+    key_grad = shifted(total, ("chip", "core"), -1).astype(jnp.float32) + shares[-1]
     return (attended, key_grad.astype(jnp.bfloat16))
 
 
 def solution(mesh):
+    positions, heads = mesh.devices.shape
+    cores = Mesh(mesh.devices.reshape(positions // 2, 2, heads), ("chip", "core", "head"))
+    split = P(("chip", "core"), "head")
     return jax.shard_map(
         local,
-        mesh=mesh,
-        in_specs=(
-            P("ctx", "head"),
-            P("ctx", "head"),
-            P("ctx", "head"),
-            P("ctx", "head"),
-            P("ctx", "head"),
-            P(),
-        ),
-        out_specs=(P("ctx", "head"), P("ctx", "head")),
+        mesh=cores,
+        in_specs=(split, split, split, split, split, P()),
+        out_specs=(split, split),
         check_vma=False,
     )

time: 458 us -> 388 us (0.85)
  waiting for transfers between devices: 359 us -> 277 us
  other arithmetic: 1.93 us -> 10.3 us
  starting transfers between devices: 13.4 us -> 18.8 us
    all_gather x4 -> x2, waiting for transfers between devices: 265 us -> 182 us  [the longest x1 113 us: local(): kv_whole = lax.all_gather(kv_piece, 'chip', axis=0, tiled=True)]
    ppermute x0 -> x7, waiting for transfers between devices: none -> 53.1 us  [the longest x1 41.9 us: gather_features(): lax.ppermute(tokens, 'head', [(i, (i + step) % count) for i in range(coun...]
    ppermute x4, waiting for transfers between devices: 91.1 us -> 42 us  [shifted(): return lax.ppermute(block, axis, route)]
    ppermute x0 -> x7, starting transfers between devices: none -> 5.09 us  [the longest x6 3.94 us: from_partner(): return lax.ppermute(block, 'core', [(0, 1), (1, 0)])]
    select_n x0 -> x6, other arithmetic: none -> 4.64 us  [the longest x3 2.33 us: in_core_order(): return (jnp.where(first, own, other), jnp.where(first, other, own))]
    dot_general x3 -> x4, matrix products: 30.1 us -> 26.7 us  [the longest x2 13.8 us: project(): others = jnp.dot(theirs, whole, preferred_element_type=jnp.float32) * factor]
  transfers between devices with their start and end apart: 8 -> 13, of which waited for: 7 -> 11; matrix products, arithmetic and copies ran while one was open for 7% -> 9% of each run, Pallas kernels for 0% -> 0%
where the time goes in v1:
time: 388 us; the launch traced here: 387 us
  waiting for transfers between devices  277 us (71%)
  Pallas kernels  38 us (10%)
  matrix products  26.7 us (7%)
  starting transfers between devices  18.8 us (5%)
  between operations  14.2 us (4%)
  other arithmetic  10.3 us (3%)
    all_gather x1, waiting for transfers between devices, local(): kv_whole = lax.all_gather(kv_piece, 'chip', axis=0, tiled=True)  113 us
    all_gather x1, waiting for transfers between devices, local(): query_whole = lax.all_gather(query_piece, 'chip', axis=0, tiled=True)  68.6 us
    ppermute x4, waiting for transfers between devices, shifted(): return lax.ppermute(block, axis, route)  42 us
    ppermute x1, waiting for transfers between devices, gather_features(): lax.ppermute(tokens, 'head', [(i, (i + step) % count) for i in range(coun...  41.9 us
    pallas_call x1, Pallas kernels, attend(): pl.pallas_call(functools.partial(attend_kernel, count, group), grid=(head...  38 us
    dot_general x2, matrix products, project(): others = jnp.dot(theirs, whole, preferred_element_type=jnp.float32) * factor  13.8 us
    ppermute x4, starting transfers between devices, shifted(): return lax.ppermute(block, axis, route)  13.6 us
    dot_general x2, matrix products, project(): mine = jnp.dot(features, whole, preferred_element_type=jnp.float32) * factor  12.9 us
  transfers between devices with their start and end apart: 13, of which 11 were waited for; matrix products, arithmetic and copies ran while one was open for 9% of the time, Pallas kernels for 0%

profile of v1, /device:TPU:13, one launch (start us, length us, event | category | flops | bytes accessed | tf_op | source)
XLA Modules:
  0.0 387.2 jit_solution(14315787976909159590)
XLA Ops:
  7.2 0.0 copy-start.3
  7.2 0.0 all-gather.3.cloned.1.call-start
  7.2 1.2 broadcast_select_fusion.14
  8.4 0.7 collective-permute-start.1
  9.1 1.1 broadcast_select_fusion.10
  10.2 0.1 collective-permute-start.2
  10.3 0.0 collective-permute-done.1
  10.3 1.1 broadcast_select_fusion.13
  11.4 0.4 collective-permute-done.2
  11.8 1.1 broadcast_select_fusion.9
  12.9 1.1 maximum_maximum_fusion
  14.0 0.0 copy-start.4
  14.0 0.0 all-gather.3.cloned.1.call-update
  14.0 0.0 all-gather.5.cloned.1.call-start
  14.1 0.0 copy-done.3
  14.1 0.1 broadcast_select_fusion.6
  14.1 0.2 collective-permute-start.3
  14.3 1.7 collective-permute-done.3
  16.1 0.1 broadcast_select_fusion.5
  16.2 1.0 pad_maximum_fusion.2
  17.2 112.9 %all-gather.3.cloned.1.call-done = bf16[3840,1024]{1,0:T(8,128)(2,1)} async-done(((bf16[480,1024]{1,0:T(8,128)(2,1)}), bf16[3840,1024]{1,0:T(8,128)(2,1)}) %all-gather.3.cloned.1.call-update) | async-done | bytes 7864336 | tf_op jit(solution)/shard_map/all_gather | solution.py:148
  130.1 0.0 all-gather.5.cloned.1.call-update
  130.1 0.0 copy-done.4
  130.1 1.1 collective-permute-start
  131.3 0.3 broadcast_in_dim.3
  131.6 0.0 copy-start.5
  131.6 0.3 constant_dynamic-update-slice_fusion.1
  131.9 41.9 %collective-permute-done = bf16[512,1920]{1,0:T(8,128)(2,1)} collective-permute-done((bf16[512,1920]{1,0:T(8,128)(2,1)S(1)}, bf16[512,1920]{1,0:T(8,128)(2,1)}, u32[]{:S(2)}, u32[]{:S(2)}) %collective-permute-start) | collective-permute-done | bytes 1966112 | tf_op jit(solution)/shard_map/ppermute | solution.py:129
  173.8 1.8 constant_dynamic-update-slice_fusion
  175.6 0.0 copy-start.2
  175.6 1.9 collective-permute-start.4
  177.5 6.4 %collective-permute-done.4 = bf16[512,3840]{1,0:T(8,128)(2,1)S(1)} collective-permute-done((bf16[512,3840]{1,0:T(8,128)(2,1)S(1)}, bf16[512,3840]{1,0:T(8,128)(2,1)S(1)}, u32[]{:S(2)}, u32[]{:S(2)}) %collective-permute-start.4) | collective-permute-done | bytes 3932192 | tf_op jit(solution)/shard_map/ppermute | solution.py:115
  183.9 0.0 copy-done.5
  183.9 0.0 copy-start.6
  183.9 4.2 %convolution_convert_fusion = bf16[512,1024]{1,0:T(8,128)(2,1)S(1)} fusion(bf16[512,3840]{1,0:T(8,128)(2,1)S(1)} %collective-permute-done.4, bf16[3840,1024]{1,0:T(8,128)(2,1)S(1)} %copy-done.5), kind=kOutput, calls=%fused_computation.6 | convolution fusion | flops 4027056128 | bytes 12845056 | tf_op jit(solution)/shard_map/dot_general | solution.py:155
  188.1 0.0 copy-done.6
  188.1 0.4 collective-permute-start.6
  188.5 2.3 collective-permute-done.6
  190.8 0.0 copy-done.2
  190.8 4.2 %broadcast_select_fusion.1 = (bf16[512,1024]{1,0:T(8,128)(2,1)S(1)}, bf16[512,1024]{1,0:T(8,128)(2,1)S(1)}) fusion(bf16[512,1024]{1,0:T(8,128)(2,1)S(1)} %collective-permute-done.6, pred[]{:T(512)S(6)} %eq.2, bf16[512,3840]{1,0:T(8,128)(2,1)S(1)} %constant_dynamic-update-slice_fusion, bf16[3840,1024]{1,0:T(8,128)(2,1)S(1)} %copy-done.5), kind=kOutput, calls=%fused_computation.9 | convolution fusion | flops 4028104704 | bytes 14942209 | tf_op jit(solution)/shard_map/dot_general | solution.py:154
  195.1 0.2 fusion
  195.2 1.7 pad_maximum_fusion.1.refs_6_.refs_9_
  196.9 5.1 %collective-permute-start.7 = (bf16[512,2048]{1,0:T(8,128)(2,1)}, bf16[512,2048]{1,0:T(8,128)(2,1)S(1)}, u32[]{:S(2)}, u32[]{:S(2)}) collective-permute-start(bf16[512,2048]{1,0:T(8,128)(2,1)} %pad_maximum_fusion.1.refs_6_.refs_9_), channel_id=1, source_target_pairs={{0,2},{2,4},{4,6},{6,8},{8,10},{10,12},{12,14},{14,16},{16,18},{18... | collective-permute-start | bytes 6291464 | tf_op jit(solution)/shard_map/ppermute | solution.py:19
  202.0 68.6 %all-gather.5.cloned.1.call-done = bf16[3840,1024]{1,0:T(8,128)(2,1)} async-done(((bf16[480,1024]{1,0:T(8,128)(2,1)}), bf16[3840,1024]{1,0:T(8,128)(2,1)}) %all-gather.5.cloned.1.call-update) | async-done | bytes 7864336 | tf_op jit(solution)/shard_map/all_gather | solution.py:150
  270.6 9.6 %multiply_convert_fusion = bf16[512,1024]{1,0:T(8,128)(2,1)} fusion(bf16[512,3840]{1,0:T(8,128)(2,1)} %copy-done.6, bf16[3840,1024]{1,0:T(8,128)(2,1)} %all-gather.5.cloned.1.call-done), kind=kOutput, calls=%fused_computation.4 | convolution fusion | flops 4027580416 | bytes 12845056 | tf_op jit(solution)/shard_map/dot_general | solution.py:155
  280.3 0.6 collective-permute-start.5
  280.9 0.0 collective-permute-done.7.refs_5_.refs_8_
  280.9 2.1 collective-permute-start.8
  283.0 0.4 collective-permute-done.5
  283.4 8.7 %broadcast_select_fusion.3 = (bf16[512,1024]{1,0:T(8,128)(2,1)S(1)}, bf16[512,1024]{1,0:T(8,128)(2,1)S(1)}) fusion(bf16[512,1024]{1,0:T(8,128)(2,1)S(1)} %collective-permute-done.5, pred[]{:T(512)S(6)} %eq.2, bf16[512,3840]{1,0:T(8,128)(2,1)} %copy-done.2, bf16[3840,1024]{1,0:T(8,128)(2,1)} %all-gather.5.cloned.1.call-done), kind=kOutput, calls=%fused_computation.11 | convolution fusion | flops 4028628992 | bytes 14942209 | tf_op jit(solution)/shard_map/dot_general | solution.py:154
  292.0 0.0 copy-start
  292.0 0.0 copy-start.1
  292.0 0.2 pad_maximum_fusion.refs_2_
  292.2 13.5 %collective-permute-done.8.refs_4_.refs_7_ = bf16[512,2048]{1,0:T(8,128)(2,1)} collective-permute-done((bf16[512,2048]{1,0:T(8,128)(2,1)S(1)}, bf16[512,2048]{1,0:T(8,128)(2,1)}, u32[]{:S(2)}, u32[]{:S(2)}) %collective-permute-start.8) | collective-permute-done | bytes 2097184 | tf_op jit(solution)/shard_map/ppermute | solution.py:19
  305.7 0.0 copy-done
  305.7 0.0 copy-done.1
  305.7 38.0 %shard_map.77 = (bf16[512,2048]{1,0:T(8,128)(2,1)}, bf16[512,1024]{1,0:T(8,128)(2,1)S(1)}, bf16[512,1024]{1,0:T(8,128)(2,1)S(1)}, f32[512,1024]{1,0:T(8,128)S(1)}) custom-call(s32[1]{0:T(128)} %bitcast.refs_0_, s32[8]{0:T(128)S(1)} %copy-done.1, bf16[512,2048]{1,0:T(8,128)(2,1)S(1)} %pad_maximum_fusion.refs_2_, bf16[512,2048]{1,0:T(8,128)(2,1)S(1)} %copy-done, ...), custom_call_target="tpu_custom_call" | custom-call | flops 12079595520 | bytes 22020096 | tf_op jit(solution)/shard_map/pallas_call | solution.py:92
  343.7 4.5 %collective-permute-start.9 = (bf16[512,1024]{1,0:T(8,128)(2,1)S(1)}, bf16[512,1024]{1,0:T(8,128)(2,1)S(1)}, u32[]{:S(2)}, u32[]{:S(2)}) collective-permute-start(bf16[512,1024]{1,0:T(8,128)(2,1)S(1)} %get-tuple-element.11), channel_id=1, source_target_pairs={{2,0},{4,2},{6,4},{8,6},{10,8},{12,10},{14,12},{16,14},{18,16},{20... | collective-permute-start | bytes 3145736 | tf_op jit(solution)/shard_map/ppermute | solution.py:19
  348.2 13.4 %collective-permute-done.9 = bf16[512,1024]{1,0:T(8,128)(2,1)S(1)} collective-permute-done((bf16[512,1024]{1,0:T(8,128)(2,1)S(1)}, bf16[512,1024]{1,0:T(8,128)(2,1)S(1)}, u32[]{:S(2)}, u32[]{:S(2)}) %collective-permute-start.9) | collective-permute-done | bytes 1048608 | tf_op jit(solution)/shard_map/ppermute | solution.py:19
  361.6 0.4 add_convert_fusion.1
  362.0 1.9 collective-permute-start.10
  363.9 15.1 %collective-permute-done.10 = bf16[512,1024]{1,0:T(8,128)(2,1)S(1)} collective-permute-done((bf16[512,1024]{1,0:T(8,128)(2,1)S(1)}, bf16[512,1024]{1,0:T(8,128)(2,1)S(1)}, u32[]{:S(2)}, u32[]{:S(2)}) %collective-permute-start.10) | collective-permute-done | bytes 1048608 | tf_op jit(solution)/shard_map/ppermute | solution.py:19
  379.0 1.4 add_convert_fusion
Async XLA Ops:
  7.2 6.9 %copy-start.3 = (bf16[240,2048]{1,0:T(8,128)(2,1)S(1)}, bf16[240,2048]{1,0:T(8,128)(2,1)}, u32[]{:S(2)}) copy-start(bf16[240,2048]{1,0:T(8,128)(2,1)} %param.7) | copy-start | bytes 2949124
  7.2 122.9 %all-gather.3.cloned.1.call-start = ((), (), s32[]{:S(2)}) async-start(), calls=%async_computation | async-start | bytes 8847360 | tf_op jit(solution)/shard_map/all_gather | solution.py:148
  8.4 1.9 collective-permute-start.1
  10.2 1.6 collective-permute-start.2
  14.0 116.1 %copy-start.4 = (bf16[512,1920]{1,0:T(8,128)(2,1)S(1)}, bf16[512,1920]{1,0:T(8,128)(2,1)}, u32[]{:S(2)}) copy-start(bf16[512,1920]{1,0:T(8,128)(2,1)} %param.6) | copy-start | bytes 5898244
  14.0 256.6 %all-gather.5.cloned.1.call-start = ((), (), s32[]{:S(2)}) async-start(), calls=%async_computation.1 | async-start | bytes 8847360 | tf_op jit(solution)/shard_map/all_gather | solution.py:150
  14.1 1.9 collective-permute-start.3
  130.1 43.6 %collective-permute-start = (bf16[512,1920]{1,0:T(8,128)(2,1)S(1)}, bf16[512,1920]{1,0:T(8,128)(2,1)}, u32[]{:S(2)}, u32[]{:S(2)}) collective-permute-start(bf16[512,1920]{1,0:T(8,128)(2,1)S(1)} %copy-done.4), channel_id=1, source_target_pairs={{0,1},{1,0},{2,3},{3,2},{4,5},{5,4},{6,7},{7,6},{8,9},{9,8},{10,11... | collective-permute-start | bytes 5898248 | tf_op jit(solution)/shard_map/ppermute | solution.py:129
  131.6 52.3 %copy-start.5 = (bf16[3840,1024]{1,0:T(8,128)(2,1)S(1)}, bf16[3840,1024]{1,0:T(8,128)(2,1)}, u32[]{:S(2)}) copy-start(bf16[3840,1024]{1,0:T(8,128)(2,1)} %all-gather.3.cloned.1.call-done) | copy-start | bytes 23592964
  175.6 15.3 %copy-start.2 = (bf16[512,3840]{1,0:T(8,128)(2,1)}, bf16[512,3840]{1,0:T(8,128)(2,1)S(1)}, u32[]{:S(2)}) copy-start(bf16[512,3840]{1,0:T(8,128)(2,1)S(1)} %constant_dynamic-update-slice_fusion) | copy-start | bytes 11796484
  175.6 8.3 %collective-permute-start.4 = (bf16[512,3840]{1,0:T(8,128)(2,1)S(1)}, bf16[512,3840]{1,0:T(8,128)(2,1)S(1)}, u32[]{:S(2)}, u32[]{:S(2)}) collective-permute-start(bf16[512,3840]{1,0:T(8,128)(2,1)S(1)} %constant_dynamic-update-slice_fusion), channel_id=1, source_target_pairs={{0,2},{2,0},{1,3},{3,1},{4,6},{6,4},{5,7},{7,5},{8,10},{10,8},{9,1... | collective-permute-start | bytes 11796488 | tf_op jit(solution)/shard_map/ppermute | solution.py:115
  183.9 4.2 %copy-start.6 = (bf16[512,3840]{1,0:T(8,128)(2,1)}, bf16[512,3840]{1,0:T(8,128)(2,1)S(1)}, u32[]{:S(2)}) copy-start(bf16[512,3840]{1,0:T(8,128)(2,1)S(1)} %collective-permute-done.4) | copy-start | bytes 11796484
  188.1 2.7 collective-permute-start.6
  196.9 84.0 %collective-permute-start.7 = (bf16[512,2048]{1,0:T(8,128)(2,1)}, bf16[512,2048]{1,0:T(8,128)(2,1)S(1)}, u32[]{:S(2)}, u32[]{:S(2)}) collective-permute-start(bf16[512,2048]{1,0:T(8,128)(2,1)} %pad_maximum_fusion.1.refs_6_.refs_9_), channel_id=1, source_target_pairs={{0,2},{2,4},{4,6},{6,8},{8,10},{10,12},{12,14},{14,16},{16,18},{18... | collective-permute-start | bytes 6291464 | tf_op jit(solution)/shard_map/ppermute | solution.py:19
  280.3 3.1 collective-permute-start.5
  280.9 24.9 %collective-permute-start.8 = (bf16[512,2048]{1,0:T(8,128)(2,1)S(1)}, bf16[512,2048]{1,0:T(8,128)(2,1)}, u32[]{:S(2)}, u32[]{:S(2)}) collective-permute-start(bf16[512,2048]{1,0:T(8,128)(2,1)S(1)} %collective-permute-done.7.refs_5_.refs_8_), channel_id=1, source_target_pairs={{0,2},{2,4},{4,6},{6,8},{8,10},{10,12},{12,14},{14,16},{16,18},{18... | collective-permute-start | bytes 6291464 | tf_op jit(solution)/shard_map/ppermute | solution.py:19
  292.0 13.7 %copy-start = (bf16[512,2048]{1,0:T(8,128)(2,1)S(1)}, bf16[512,2048]{1,0:T(8,128)(2,1)}, u32[]{:S(2)}) copy-start(bf16[512,2048]{1,0:T(8,128)(2,1)} %refs_3_.1) | copy-start | bytes 6291460
  292.0 13.7 %copy-start.1 = (s32[8]{0:T(128)S(1)}, s32[8]{0:T(128)}, u32[]{:S(2)}) copy-start(s32[8]{0:T(128)} %refs_1_.1) | copy-start | bytes 100
  343.7 17.9 %collective-permute-start.9 = (bf16[512,1024]{1,0:T(8,128)(2,1)S(1)}, bf16[512,1024]{1,0:T(8,128)(2,1)S(1)}, u32[]{:S(2)}, u32[]{:S(2)}) collective-permute-start(bf16[512,1024]{1,0:T(8,128)(2,1)S(1)} %get-tuple-element.11), channel_id=1, source_target_pairs={{2,0},{4,2},{6,4},{8,6},{10,8},{12,10},{14,12},{16,14},{18,16},{20... | collective-permute-start | bytes 3145736 | tf_op jit(solution)/shard_map/ppermute | solution.py:19
  362.0 17.0 %collective-permute-start.10 = (bf16[512,1024]{1,0:T(8,128)(2,1)S(1)}, bf16[512,1024]{1,0:T(8,128)(2,1)S(1)}, u32[]{:S(2)}, u32[]{:S(2)}) collective-permute-start(bf16[512,1024]{1,0:T(8,128)(2,1)S(1)} %add_convert_fusion.1), channel_id=1, source_target_pairs={{2,0},{4,2},{6,4},{8,6},{10,8},{12,10},{14,12},{16,14},{18,16},{20... | collective-permute-start | bytes 3145736 | tf_op jit(solution)/shard_map/ppermute | solution.py:19
Sparse Core Ops, SparseCore 0:
  14.1 115.9 all-gather.2
  132.9 137.7 all-gather.4

commit v2 on v1

--- a/solution.py
+++ b/solution.py
@@ -146,7 +146,7 @@
     features = gather_features(tokens)
     kv_piece = jnp.concatenate([half_columns(key_matrix), half_columns(value_matrix)], axis=1)
     kv_whole = lax.all_gather(kv_piece, "chip", axis=0, tiled=True)
-    kv_whole, query_piece = lax.optimization_barrier((kv_whole, half_columns(w_query)))
+    query_piece = half_columns(w_query) + features[:1, :1] * 0 + features[:1, -1:] * 0
     query_whole = lax.all_gather(query_piece, "chip", axis=0, tiled=True)
     theirs = from_partner(features)
 
@@ -163,13 +163,19 @@
         joined = [shifted(joined[0], ("chip", "core"), 1)] + joined
     query = jnp.concatenate(project(query_whole, 0.0625), axis=1)
     lead = (lax.axis_index(("chip", "core")) * rows_here).astype(jnp.int32).reshape(1)
-    attended, shares = attend(query, d_attended, joined, lead, doc_lengths, 0, kv_heads)
-    total = shares[0]
-    for share in shares[1:-1]:
-        moved = shifted(total, ("chip", "core"), -1).astype(jnp.float32)
-        total = (moved + share.astype(jnp.float32)).astype(jnp.bfloat16)
-    key_grad = shifted(total, ("chip", "core"), -1).astype(jnp.float32) + shares[-1]
-    return (attended, key_grad.astype(jnp.bfloat16))
+    parts = 2 if kv_heads % 2 == 0 else 1
+    heads = kv_heads // parts
+    outs, grads = [], []
+    for part in range(parts):
+        out, shares = attend(query, d_attended, joined, lead, doc_lengths, part * heads, heads)
+        total = shares[0]
+        for share in shares[1:-1]:
+            moved = shifted(total, ("chip", "core"), -1).astype(jnp.float32)
+            total = (moved + share.astype(jnp.float32)).astype(jnp.bfloat16)
+        key_grad = shifted(total, ("chip", "core"), -1).astype(jnp.float32) + shares[-1]
+        outs.append(out)
+        grads.append(key_grad.astype(jnp.bfloat16))
+    return (jnp.concatenate(outs, axis=1), jnp.concatenate(grads, axis=1))
 
 
 def solution(mesh):

time: 388 us -> 376 us (0.969)
  waiting for transfers between devices: 277 us -> 247 us
  starting transfers between devices: 18.8 us -> 26.3 us
  matrix products: 26.7 us -> 31.3 us
    all_gather x1, waiting for transfers between devices: 113 us -> 57.1 us  [local(): kv_whole = lax.all_gather(kv_piece, 'chip', axis=0, tiled=True)]
    all_gather x1, waiting for transfers between devices: 68.6 us -> 111 us  [local(): query_whole = lax.all_gather(query_piece, 'chip', axis=0, tiled=True)]
    ppermute x4 -> x6, waiting for transfers between devices: 42 us -> 28.4 us  [shifted(): return lax.ppermute(block, axis, route)]
    ppermute x4 -> x6, starting transfers between devices: 13.6 us -> 21.3 us  [shifted(): return lax.ppermute(block, axis, route)]
    dot_general x2, matrix products: 13.8 us -> 18.4 us  [project(): others = jnp.dot(theirs, whole, preferred_element_type=jnp.float32) * factor]
    pallas_call x1 -> x2, Pallas kernels: 38 us -> 38.4 us  [attend(): pl.pallas_call(functools.partial(attend_kernel, count, group), grid=(head...]
  transfers between devices with their start and end apart: 13 -> 15, of which waited for: 11 -> 11; matrix products, arithmetic and copies ran while one was open for 9% -> 11% of each run, Pallas kernels for 0% -> 5%
where the time goes in v2:
time: 376 us; the launch traced here: 375 us
  waiting for transfers between devices  247 us (66%)
  Pallas kernels  38.4 us (10%)
  matrix products  31.3 us (8%)
  starting transfers between devices  26.3 us (7%)
  between operations  15.5 us (4%)
  other arithmetic  11.5 us (3%)
  local copies, waits for them, and re-layouts  4.97 us (1%)
    all_gather x1, waiting for transfers between devices, local(): query_whole = lax.all_gather(query_piece, 'chip', axis=0, tiled=True)  111 us
    all_gather x1, waiting for transfers between devices, local(): kv_whole = lax.all_gather(kv_piece, 'chip', axis=0, tiled=True)  57.1 us
    ppermute x1, waiting for transfers between devices, gather_features(): lax.ppermute(tokens, 'head', [(i, (i + step) % count) for i in range(coun...  40.1 us
    pallas_call x2, Pallas kernels, attend(): pl.pallas_call(functools.partial(attend_kernel, count, group), grid=(head...  38.4 us
    ppermute x6, waiting for transfers between devices, shifted(): return lax.ppermute(block, axis, route)  28.4 us
    ppermute x6, starting transfers between devices, shifted(): return lax.ppermute(block, axis, route)  21.3 us
    dot_general x2, matrix products, project(): others = jnp.dot(theirs, whole, preferred_element_type=jnp.float32) * factor  18.4 us
    dot_general x2, matrix products, project(): mine = jnp.dot(features, whole, preferred_element_type=jnp.float32) * factor  12.9 us
  transfers between devices with their start and end apart: 15, of which 11 were waited for; matrix products, arithmetic and copies ran while one was open for 11% of the time, Pallas kernels for 5%

profile of v2, /device:TPU:13, one launch (start us, length us, event | category | flops | bytes accessed | tf_op | source)
XLA Modules:
  0.0 375.2 jit_solution(3235501063787510504)
XLA Ops:
  7.2 0.0 copy-start.5
  7.2 0.0 copy-start.4
  7.2 0.0 all-gather.5.cloned.1.call-start
  7.2 1.2 broadcast_select_fusion.10
  8.5 0.7 collective-permute-start.5
  9.2 1.1 broadcast_select_fusion.14
  10.3 0.1 collective-permute-start.4
  10.4 0.0 collective-permute-done.5
  10.4 1.1 broadcast_select_fusion.9
  11.5 0.4 collective-permute-done.4
  11.9 1.1 broadcast_select_fusion.13
  13.0 1.1 maximum_maximum_fusion
  14.1 0.0 all-gather.5.cloned.1.call-update
  14.1 0.0 all-gather.3.cloned.1.call-start
  14.2 1.3 collective-permute-start
  15.4 0.8 broadcast_select_fusion.6
  16.3 0.4 collective-permute-start.1
  16.7 0.3 broadcast_in_dim.3
  17.0 0.3 constant_dynamic-update-slice_fusion.1
  17.3 1.1 collective-permute-done.1
  18.4 0.1 broadcast_select_fusion.5
  18.5 40.1 %collective-permute-done = bf16[512,1920]{1,0:T(8,128)(2,1)} collective-permute-done((bf16[512,1920]{1,0:T(8,128)(2,1)S(1)}, bf16[512,1920]{1,0:T(8,128)(2,1)}, u32[]{:S(2)}, u32[]{:S(2)}) %collective-permute-start) | collective-permute-done | bytes 1966112 | tf_op jit(solution)/shard_map/ppermute | solution.py:129
  58.6 1.8 constant_dynamic-update-slice_fusion
  60.5 1.9 copy-done.2
  62.3 0.5 fusion.1
  64.1 1.2 fusion
  65.3 0.0 all-gather.3.cloned.1.call-update
  65.3 1.0 collective-permute-start.2
  66.3 6.8 %collective-permute-done.2 = bf16[512,3840]{1,0:T(8,128)(2,1)} collective-permute-done((bf16[512,3840]{1,0:T(8,128)(2,1)}, bf16[512,3840]{1,0:T(8,128)(2,1)}, u32[]{:S(2)}, u32[]{:S(2)}) %collective-permute-start.2) | collective-permute-done | bytes 3932192 | tf_op jit(solution)/shard_map/ppermute | solution.py:115
  73.1 57.1 %all-gather.5.cloned.1.call-done = bf16[3840,1024]{1,0:T(8,128)(2,1)} async-done(((bf16[480,1024]{1,0:T(8,128)(2,1)}), bf16[3840,1024]{1,0:T(8,128)(2,1)}) %all-gather.5.cloned.1.call-update) | async-done | bytes 7864336 | tf_op jit(solution)/shard_map/all_gather | solution.py:148
  130.2 8.8 %convolution_convert_fusion = bf16[512,1024]{1,0:T(8,128)(2,1)S(1)} fusion(bf16[512,3840]{1,0:T(8,128)(2,1)} %collective-permute-done.2, bf16[3840,1024]{1,0:T(8,128)(2,1)} %all-gather.5.cloned.1.call-done), kind=kOutput, calls=%fused_computation.5 | convolution fusion | flops 4027056128 | bytes 12845056 | tf_op jit(solution)/shard_map/dot_general | solution.py:155
  139.0 1.0 collective-permute-start.6
  140.0 2.3 collective-permute-done.6
  142.2 4.2 %broadcast_select_fusion.1 = (bf16[512,1024]{1,0:T(8,128)(2,1)S(1)}, bf16[512,1024]{1,0:T(8,128)(2,1)S(1)}) fusion(bf16[512,1024]{1,0:T(8,128)(2,1)S(1)} %collective-permute-done.6, pred[]{:T(512)S(6)} %eq.2, bf16[512,3840]{1,0:T(8,128)(2,1)S(1)} %copy-done.3, bf16[3840,1024]{1,0:T(8,128)(2,1)S(1)} %copy-done.6), kind=kOutput, calls=%fused_computation.13 | convolution fusion | flops 4028104704 | bytes 14942209 | tf_op jit(solution)/shard_map/dot_general | solution.py:154
  146.5 0.2 fusion.2
  146.6 0.3 pad_maximum_fusion.1.refs_6_.refs_9_
  146.9 5.3 %collective-permute-start.7 = (bf16[512,2048]{1,0:T(8,128)(2,1)S(1)}, bf16[512,2048]{1,0:T(8,128)(2,1)}, u32[]{:S(2)}, u32[]{:S(2)}) collective-permute-start(bf16[512,2048]{1,0:T(8,128)(2,1)S(1)} %pad_maximum_fusion.1.refs_6_.refs_9_), channel_id=1, source_target_pairs={{0,2},{2,4},{4,6},{6,8},{8,10},{10,12},{12,14},{14,16},{16,18},{18... | collective-permute-start | bytes 6291464 | tf_op jit(solution)/shard_map/ppermute | solution.py:19
  152.3 111.0 %all-gather.3.cloned.1.call-done = bf16[3840,1024]{1,0:T(8,128)(2,1)} async-done(((bf16[480,1024]{1,0:T(8,128)(2,1)}), bf16[3840,1024]{1,0:T(8,128)(2,1)}) %all-gather.3.cloned.1.call-update) | async-done | bytes 7864336 | tf_op jit(solution)/shard_map/all_gather | solution.py:150
  263.3 9.6 %multiply_convert_fusion = bf16[512,1024]{1,0:T(8,128)(2,1)} fusion(bf16[512,3840]{1,0:T(8,128)(2,1)} %collective-permute-done.2, bf16[3840,1024]{1,0:T(8,128)(2,1)} %all-gather.3.cloned.1.call-done), kind=kOutput, calls=%fused_computation.3 | convolution fusion | flops 4027580416 | bytes 12845056 | tf_op jit(solution)/shard_map/dot_general | solution.py:155
  272.9 0.5 collective-permute-start.3
  273.4 0.0 collective-permute-done.7.refs_5_.refs_8_
  273.4 6.6 %collective-permute-start.8 = (bf16[512,2048]{1,0:T(8,128)(2,1)}, bf16[512,2048]{1,0:T(8,128)(2,1)}, u32[]{:S(2)}, u32[]{:S(2)}) collective-permute-start(bf16[512,2048]{1,0:T(8,128)(2,1)} %collective-permute-done.7.refs_5_.refs_8_), channel_id=1, source_target_pairs={{0,2},{2,4},{4,6},{6,8},{8,10},{10,12},{12,14},{14,16},{16,18},{18... | collective-permute-start | bytes 6291464 | tf_op jit(solution)/shard_map/ppermute | solution.py:19
  280.0 0.0 collective-permute-done.3
  280.0 8.7 %broadcast_select_fusion.3 = (bf16[512,1024]{1,0:T(8,128)(2,1)S(1)}, bf16[512,1024]{1,0:T(8,128)(2,1)S(1)}) fusion(bf16[512,1024]{1,0:T(8,128)(2,1)S(1)} %collective-permute-done.3, pred[]{:T(512)S(6)} %eq.2, bf16[512,3840]{1,0:T(8,128)(2,1)} %copy-done.2, bf16[3840,1024]{1,0:T(8,128)(2,1)} %all-gather.3.cloned.1.call-done), kind=kOutput, calls=%fused_computation.15 | convolution fusion | flops 4028628992 | bytes 14942209 | tf_op jit(solution)/shard_map/dot_general | solution.py:154
  288.6 0.0 copy-start
  288.6 0.0 copy-start.1
  288.7 0.2 pad_maximum_fusion.refs_2_
  288.8 14.2 %collective-permute-done.8.refs_4_.refs_7_ = bf16[512,2048]{1,0:T(8,128)(2,1)} collective-permute-done((bf16[512,2048]{1,0:T(8,128)(2,1)}, bf16[512,2048]{1,0:T(8,128)(2,1)}, u32[]{:S(2)}, u32[]{:S(2)}) %collective-permute-start.8) | collective-permute-done | bytes 2097184 | tf_op jit(solution)/shard_map/ppermute | solution.py:19
  303.0 19.2 %shard_map.78 = (bf16[512,1024]{1,0:T(8,128)(2,1)S(1)}, bf16[512,512]{1,0:T(8,128)(2,1)S(1)}, bf16[512,512]{1,0:T(8,128)(2,1)S(1)}, f32[512,512]{1,0:T(8,128)S(1)}) custom-call(s32[1]{0:T(128)} %bitcast.refs_0_, s32[8]{0:T(128)S(1)} %copy-done.1, bf16[512,2048]{1,0:T(8,128)(2,1)S(1)} %pad_maximum_fusion.refs_2_, bf16[512,2048]{1,0:T(8,128)(2,1)S(1)} %copy-done, ...), custom_call_target="tpu_custom_call" | custom-call | flops 6039797760 | bytes 11010048 | tf_op jit(solution)/shard_map/pallas_call | solution.py:92
  322.3 1.9 collective-permute-start.11
  324.2 19.2 %shard_map.77 = (bf16[512,1024]{1,0:T(8,128)(2,1)S(1)}, bf16[512,512]{1,0:T(8,128)(2,1)S(1)}, bf16[512,512]{1,0:T(8,128)(2,1)S(1)}, f32[512,512]{1,0:T(8,128)S(1)}) custom-call(s32[1]{0:T(128)} %bitcast.refs_0_, s32[8]{0:T(128)S(1)} %copy-done.1, bf16[512,2048]{1,0:T(8,128)(2,1)S(1)} %pad_maximum_fusion.refs_2_, bf16[512,2048]{1,0:T(8,128)(2,1)S(1)} %copy-done, ...), custom_call_target="tpu_custom_call" | custom-call | flops 6039797760 | bytes 11010048 | tf_op jit(solution)/shard_map/pallas_call | solution.py:92
  343.4 1.9 collective-permute-start.9
  345.3 0.0 collective-permute-done.11
  345.3 0.1 add_convert_fusion.1
  345.5 3.6 collective-permute-start.12
  349.1 6.4 %collective-permute-done.9 = bf16[512,512]{1,0:T(8,128)(2,1)S(1)} collective-permute-done((bf16[512,512]{1,0:T(8,128)(2,1)S(1)}, bf16[512,512]{1,0:T(8,128)(2,1)S(1)}, u32[]{:S(2)}, u32[]{:S(2)}) %collective-permute-start.9) | collective-permute-done | bytes 524320 | tf_op jit(solution)/shard_map/ppermute | solution.py:19
  355.5 0.1 add_convert_fusion.3
  355.7 1.9 collective-permute-start.10
  357.6 1.5 pad_maximum_fusion.2
  359.1 2.0 collective-permute-done.12
  361.2 0.2 add_convert_fusion
  361.4 5.7 %collective-permute-done.10 = bf16[512,512]{1,0:T(8,128)(2,1)S(1)} collective-permute-done((bf16[512,512]{1,0:T(8,128)(2,1)S(1)}, bf16[512,512]{1,0:T(8,128)(2,1)S(1)}, u32[]{:S(2)}, u32[]{:S(2)}) %collective-permute-start.10) | collective-permute-done | bytes 524320 | tf_op jit(solution)/shard_map/ppermute | solution.py:19
  367.1 0.2 add_convert_fusion.2
  367.3 1.1 pad_maximum_fusion.3
  (9 shorter events, 0.0 us)
Async XLA Ops:
  7.2 7.0 %copy-start.5 = (bf16[512,1920]{1,0:T(8,128)(2,1)S(1)}, bf16[512,1920]{1,0:T(8,128)(2,1)}, u32[]{:S(2)}) copy-start(bf16[512,1920]{1,0:T(8,128)(2,1)} %param.6) | copy-start | bytes 5898244
  7.2 8.3 %copy-start.4 = (bf16[240,2048]{1,0:T(8,128)(2,1)S(1)}, bf16[240,2048]{1,0:T(8,128)(2,1)}, u32[]{:S(2)}) copy-start(bf16[240,2048]{1,0:T(8,128)(2,1)} %param.7) | copy-start | bytes 2949124
  7.2 123.0 %all-gather.5.cloned.1.call-start = ((), (), s32[]{:S(2)}) async-start(), calls=%async_computation.1 | async-start | bytes 8847360 | tf_op jit(solution)/shard_map/all_gather | solution.py:148
  8.5 1.9 collective-permute-start.5
  10.3 1.6 collective-permute-start.4
  14.1 249.2 %all-gather.3.cloned.1.call-start = ((), (), s32[]{:S(2)}) async-start(), calls=%async_computation | async-start | bytes 8847360 | tf_op jit(solution)/shard_map/all_gather | solution.py:150
  14.2 44.5 %collective-permute-start = (bf16[512,1920]{1,0:T(8,128)(2,1)S(1)}, bf16[512,1920]{1,0:T(8,128)(2,1)}, u32[]{:S(2)}, u32[]{:S(2)}) collective-permute-start(bf16[512,1920]{1,0:T(8,128)(2,1)S(1)} %copy-done.5), channel_id=1, source_target_pairs={{0,1},{1,0},{2,3},{3,2},{4,5},{5,4},{6,7},{7,6},{8,9},{9,8},{10,11... | collective-permute-start | bytes 5898248 | tf_op jit(solution)/shard_map/ppermute | solution.py:129
  16.3 2.1 collective-permute-start.1
  60.4 1.9 copy-start.2
  65.3 7.8 %collective-permute-start.2 = (bf16[512,3840]{1,0:T(8,128)(2,1)}, bf16[512,3840]{1,0:T(8,128)(2,1)}, u32[]{:S(2)}, u32[]{:S(2)}) collective-permute-start(bf16[512,3840]{1,0:T(8,128)(2,1)} %copy-done.2), channel_id=1, source_target_pairs={{0,2},{2,0},{1,3},{3,1},{4,6},{6,4},{5,7},{7,5},{8,10},{10,8},{9,1... | collective-permute-start | bytes 11796488 | tf_op jit(solution)/shard_map/ppermute | solution.py:115
  130.2 12.0 %copy-start.3 = (bf16[512,3840]{1,0:T(8,128)(2,1)S(1)}, bf16[512,3840]{1,0:T(8,128)(2,1)}, u32[]{:S(2)}) copy-start(bf16[512,3840]{1,0:T(8,128)(2,1)} %copy-done.2) | copy-start | bytes 11796484
  130.2 12.0 %copy-start.6 = (bf16[3840,1024]{1,0:T(8,128)(2,1)S(1)}, bf16[3840,1024]{1,0:T(8,128)(2,1)}, u32[]{:S(2)}) copy-start(bf16[3840,1024]{1,0:T(8,128)(2,1)} %all-gather.5.cloned.1.call-done) | copy-start | bytes 23592964
  139.0 3.3 collective-permute-start.6
  146.9 126.4 %collective-permute-start.7 = (bf16[512,2048]{1,0:T(8,128)(2,1)S(1)}, bf16[512,2048]{1,0:T(8,128)(2,1)}, u32[]{:S(2)}, u32[]{:S(2)}) collective-permute-start(bf16[512,2048]{1,0:T(8,128)(2,1)S(1)} %pad_maximum_fusion.1.refs_6_.refs_9_), channel_id=1, source_target_pairs={{0,2},{2,4},{4,6},{6,8},{8,10},{10,12},{12,14},{14,16},{16,18},{18... | collective-permute-start | bytes 6291464 | tf_op jit(solution)/shard_map/ppermute | solution.py:19
  272.9 7.1 %collective-permute-start.3 = (bf16[512,1024]{1,0:T(8,128)(2,1)}, bf16[512,1024]{1,0:T(8,128)(2,1)S(1)}, u32[]{:S(2)}, u32[]{:S(2)}) collective-permute-start(bf16[512,1024]{1,0:T(8,128)(2,1)} %multiply_convert_fusion), channel_id=1, source_target_pairs={{0,2},{2,0},{1,3},{3,1},{4,6},{6,4},{5,7},{7,5},{8,10},{10,8},{9,1... | collective-permute-start | bytes 3145736 | tf_op jit(solution)/shard_map/ppermute | solution.py:115
  273.4 29.7 %collective-permute-start.8 = (bf16[512,2048]{1,0:T(8,128)(2,1)}, bf16[512,2048]{1,0:T(8,128)(2,1)}, u32[]{:S(2)}, u32[]{:S(2)}) collective-permute-start(bf16[512,2048]{1,0:T(8,128)(2,1)} %collective-permute-done.7.refs_5_.refs_8_), channel_id=1, source_target_pairs={{0,2},{2,4},{4,6},{6,8},{8,10},{10,12},{12,14},{14,16},{16,18},{18... | collective-permute-start | bytes 6291464 | tf_op jit(solution)/shard_map/ppermute | solution.py:19
  288.6 14.4 %copy-start = (bf16[512,2048]{1,0:T(8,128)(2,1)S(1)}, bf16[512,2048]{1,0:T(8,128)(2,1)}, u32[]{:S(2)}) copy-start(bf16[512,2048]{1,0:T(8,128)(2,1)} %refs_3_.3) | copy-start | bytes 6291460
  288.6 14.4 %copy-start.1 = (s32[8]{0:T(128)S(1)}, s32[8]{0:T(128)}, u32[]{:S(2)}) copy-start(s32[8]{0:T(128)} %refs_1_.3) | copy-start | bytes 100
  322.3 23.1 %collective-permute-start.11 = (bf16[512,512]{1,0:T(8,128)(2,1)S(1)}, bf16[512,512]{1,0:T(8,128)(2,1)S(1)}, u32[]{:S(2)}, u32[]{:S(2)}) collective-permute-start(bf16[512,512]{1,0:T(8,128)(2,1)S(1)} %get-tuple-element.15), channel_id=1, source_target_pairs={{2,0},{4,2},{6,4},{8,6},{10,8},{12,10},{14,12},{16,14},{18,16},{20... | collective-permute-start | bytes 1572872 | tf_op jit(solution)/shard_map/ppermute | solution.py:19
  343.4 12.1 %collective-permute-start.9 = (bf16[512,512]{1,0:T(8,128)(2,1)S(1)}, bf16[512,512]{1,0:T(8,128)(2,1)S(1)}, u32[]{:S(2)}, u32[]{:S(2)}) collective-permute-start(bf16[512,512]{1,0:T(8,128)(2,1)S(1)} %get-tuple-element.12), channel_id=1, source_target_pairs={{2,0},{4,2},{6,4},{8,6},{10,8},{12,10},{14,12},{16,14},{18,16},{20... | collective-permute-start | bytes 1572872 | tf_op jit(solution)/shard_map/ppermute | solution.py:19
  345.5 15.7 %collective-permute-start.12 = (bf16[512,512]{1,0:T(8,128)(2,1)S(1)}, bf16[512,512]{1,0:T(8,128)(2,1)S(1)}, u32[]{:S(2)}, u32[]{:S(2)}) collective-permute-start(bf16[512,512]{1,0:T(8,128)(2,1)S(1)} %add_convert_fusion.1), channel_id=1, source_target_pairs={{2,0},{4,2},{6,4},{8,6},{10,8},{12,10},{14,12},{16,14},{18,16},{20... | collective-permute-start | bytes 1572872 | tf_op jit(solution)/shard_map/ppermute | solution.py:19
  355.7 11.4 %collective-permute-start.10 = (bf16[512,512]{1,0:T(8,128)(2,1)S(1)}, bf16[512,512]{1,0:T(8,128)(2,1)S(1)}, u32[]{:S(2)}, u32[]{:S(2)}) collective-permute-start(bf16[512,512]{1,0:T(8,128)(2,1)S(1)} %add_convert_fusion.3), channel_id=1, source_target_pairs={{2,0},{4,2},{6,4},{8,6},{10,8},{12,10},{14,12},{16,14},{18,16},{20... | collective-permute-start | bytes 1572872 | tf_op jit(solution)/shard_map/ppermute | solution.py:19
Sparse Core Ops, SparseCore 0:
  14.2 115.9 all-gather.4
  133.0 130.2 all-gather.2

commit v3 on v2

--- a/solution.py
+++ b/solution.py
@@ -10,7 +10,7 @@
 
 HEAD_SIZE = 256
 WINDOW = 1024
-TILE = 128
+TILE = 256
 
 
 def shifted(block, axis, distance):
@@ -82,7 +82,8 @@
     rows = query.shape[0]
     count = len(joined)
     kv_heads = joined[0].shape[1] // (2 * HEAD_SIZE)
-    group = query.shape[1] // (kv_heads * HEAD_SIZE)
+    group = grad_rows.shape[1] // (kv_heads * HEAD_SIZE)
+    query_spec = pl.BlockSpec((rows, group * HEAD_SIZE), lambda g: (0, g))
     wide = pl.BlockSpec((rows, group * HEAD_SIZE), lambda g: (0, first_head + g))
     key_spec = pl.BlockSpec((rows, HEAD_SIZE), lambda g: (0, first_head + g))
     value_spec = pl.BlockSpec((rows, HEAD_SIZE), lambda g: (0, kv_heads + first_head + g))
@@ -92,7 +93,7 @@
     outs = pl.pallas_call(
         functools.partial(attend_kernel, count, group),
         grid=(heads,),
-        in_specs=[scalars, scalars, wide, wide] + [key_spec] * count + [value_spec] * count,
+        in_specs=[scalars, scalars, query_spec, wide] + [key_spec] * count + [value_spec] * count,
         out_specs=[pl.BlockSpec((rows, group * HEAD_SIZE), lambda g: (0, g))] + [sum_spec] * count,
         out_shape=[jax.ShapeDtypeStruct((rows, heads * group * HEAD_SIZE), jnp.bfloat16)]
         + [jax.ShapeDtypeStruct((rows, heads * HEAD_SIZE), kind) for kind in kinds],
@@ -161,13 +162,15 @@
     joined = [jnp.concatenate([left[:, :half], right[:, :half], left[:, half:], right[:, half:]], axis=1)]
     for _ in range(blocks):
         joined = [shifted(joined[0], ("chip", "core"), 1)] + joined
-    query = jnp.concatenate(project(query_whole, 0.0625), axis=1)
+    queries = project(query_whole, 0.0625)
     lead = (lax.axis_index(("chip", "core")) * rows_here).astype(jnp.int32).reshape(1)
     parts = 2 if kv_heads % 2 == 0 else 1
     heads = kv_heads // parts
+    if parts == 1:
+        queries = [jnp.concatenate(queries, axis=1)]
     outs, grads = [], []
     for part in range(parts):
-        out, shares = attend(query, d_attended, joined, lead, doc_lengths, part * heads, heads)
+        out, shares = attend(queries[part], d_attended, joined, lead, doc_lengths, part * heads, heads)
         total = shares[0]
         for share in shares[1:-1]:
             moved = shifted(total, ("chip", "core"), -1).astype(jnp.float32)

time: 376 us -> 364 us (0.968)
  Pallas kernels: 38.4 us -> 26.7 us
    pallas_call x2, Pallas kernels: 38.4 us -> 26.7 us  [attend(): pl.pallas_call(functools.partial(attend_kernel, count, group), grid=(head...]
  transfers between devices with their start and end apart: 15 -> 15, of which waited for: 11 -> 11; matrix products, arithmetic and copies ran while one was open for 11% -> 11% of each run, Pallas kernels for 5% -> 4%
where the time goes in v3:
time: 364 us; the launch traced here: 363 us
  waiting for transfers between devices  247 us (68%)
  matrix products  31.4 us (9%)
  Pallas kernels  26.7 us (7%)
  starting transfers between devices  26.3 us (7%)
  between operations  15.5 us (4%)
  other arithmetic  11.3 us (3%)
  local copies, waits for them, and re-layouts  4.97 us (1%)
    all_gather x1, waiting for transfers between devices, local(): query_whole = lax.all_gather(query_piece, 'chip', axis=0, tiled=True)  111 us
    all_gather x1, waiting for transfers between devices, local(): kv_whole = lax.all_gather(kv_piece, 'chip', axis=0, tiled=True)  57.1 us
    ppermute x1, waiting for transfers between devices, gather_features(): lax.ppermute(tokens, 'head', [(i, (i + step) % count) for i in range(coun...  40.1 us
    ppermute x6, waiting for transfers between devices, shifted(): return lax.ppermute(block, axis, route)  28.5 us
    pallas_call x2, Pallas kernels, attend(): pl.pallas_call(functools.partial(attend_kernel, count, group), grid=(head...  26.7 us
    ppermute x6, starting transfers between devices, shifted(): return lax.ppermute(block, axis, route)  21.3 us
    dot_general x2, matrix products, project(): others = jnp.dot(theirs, whole, preferred_element_type=jnp.float32) * factor  18.4 us
    dot_general x2, matrix products, project(): mine = jnp.dot(features, whole, preferred_element_type=jnp.float32) * factor  13 us
  transfers between devices with their start and end apart: 15, of which 11 were waited for; matrix products, arithmetic and copies ran while one was open for 11% of the time, Pallas kernels for 4%

profile of v3, /device:TPU:13, one launch (start us, length us, event | category | flops | bytes accessed | tf_op | source)
XLA Modules:
  0.0 363.5 jit_solution(5531023449692379403)
XLA Ops:
  7.2 0.0 all-gather.5.cloned.1.call-start
  7.2 1.2 broadcast_select_fusion.10
  8.5 0.7 collective-permute-start.5
  9.2 1.1 broadcast_select_fusion.14
  10.3 0.1 collective-permute-start.4
  10.4 0.0 collective-permute-done.5
  10.4 1.1 broadcast_select_fusion.9
  11.5 0.4 collective-permute-done.4
  11.9 1.1 broadcast_select_fusion.13
  13.0 1.1 maximum_maximum_fusion
  14.1 0.0 all-gather.5.cloned.1.call-update
  14.1 0.0 all-gather.3.cloned.1.call-start
  14.2 0.0 copy-done.5
  14.2 1.3 collective-permute-start
  15.4 0.0 copy-done.4
  15.4 0.8 broadcast_select_fusion.6
  16.3 0.4 collective-permute-start.1
  16.7 0.3 broadcast_in_dim.3
  17.0 0.3 constant_dynamic-update-slice_fusion.1
  17.3 1.1 collective-permute-done.1
  18.4 0.1 broadcast_select_fusion.5
  18.5 40.1 %collective-permute-done = bf16[512,1920]{1,0:T(8,128)(2,1)} collective-permute-done((bf16[512,1920]{1,0:T(8,128)(2,1)S(1)}, bf16[512,1920]{1,0:T(8,128)(2,1)}, u32[]{:S(2)}, u32[]{:S(2)}) %collective-permute-start) | collective-permute-done | bytes 1966112 | tf_op jit(solution)/shard_map/ppermute | solution.py:130
  58.6 1.8 constant_dynamic-update-slice_fusion
  60.5 1.9 copy-done.2
  62.3 0.5 fusion.1
  64.1 1.2 fusion
  65.3 0.0 all-gather.3.cloned.1.call-update
  65.3 1.0 collective-permute-start.2
  66.3 6.8 %collective-permute-done.2 = bf16[512,3840]{1,0:T(8,128)(2,1)} collective-permute-done((bf16[512,3840]{1,0:T(8,128)(2,1)}, bf16[512,3840]{1,0:T(8,128)(2,1)}, u32[]{:S(2)}, u32[]{:S(2)}) %collective-permute-start.2) | collective-permute-done | bytes 3932192 | tf_op jit(solution)/shard_map/ppermute | solution.py:116
  73.1 57.1 %all-gather.5.cloned.1.call-done = bf16[3840,1024]{1,0:T(8,128)(2,1)} async-done(((bf16[480,1024]{1,0:T(8,128)(2,1)}), bf16[3840,1024]{1,0:T(8,128)(2,1)}) %all-gather.5.cloned.1.call-update) | async-done | bytes 7864336 | tf_op jit(solution)/shard_map/all_gather | solution.py:149
  130.2 8.8 %convolution_convert_fusion = bf16[512,1024]{1,0:T(8,128)(2,1)S(1)} fusion(bf16[512,3840]{1,0:T(8,128)(2,1)} %collective-permute-done.2, bf16[3840,1024]{1,0:T(8,128)(2,1)} %all-gather.5.cloned.1.call-done), kind=kOutput, calls=%fused_computation.4 | convolution fusion | flops 4027056128 | bytes 12845056 | tf_op jit(solution)/shard_map/dot_general | solution.py:156
  139.0 1.0 collective-permute-start.6
  140.0 2.3 collective-permute-done.6
  142.2 0.0 copy-done.6
  142.2 4.2 %broadcast_select_fusion.2 = (bf16[512,1024]{1,0:T(8,128)(2,1)S(1)}, bf16[512,1024]{1,0:T(8,128)(2,1)S(1)}) fusion(bf16[512,1024]{1,0:T(8,128)(2,1)S(1)} %collective-permute-done.6, pred[]{:T(512)S(6)} %eq.2, bf16[512,3840]{1,0:T(8,128)(2,1)S(1)} %copy-done.3, bf16[3840,1024]{1,0:T(8,128)(2,1)S(1)} %copy-done.6), kind=kOutput, calls=%fused_computation.13 | convolution fusion | flops 4028104704 | bytes 14942209 | tf_op jit(solution)/shard_map/dot_general | solution.py:155
  146.5 0.2 fusion.2
  146.6 0.3 pad_maximum_fusion.refs_6_.refs_9_
  146.9 5.3 %collective-permute-start.7 = (bf16[512,2048]{1,0:T(8,128)(2,1)S(1)}, bf16[512,2048]{1,0:T(8,128)(2,1)}, u32[]{:S(2)}, u32[]{:S(2)}) collective-permute-start(bf16[512,2048]{1,0:T(8,128)(2,1)S(1)} %pad_maximum_fusion.refs_6_.refs_9_), channel_id=1, source_target_pairs={{0,2},{2,4},{4,6},{6,8},{8,10},{10,12},{12,14},{14,16},{16,18},{18... | collective-permute-start | bytes 6291464 | tf_op jit(solution)/shard_map/ppermute | solution.py:19
  152.3 111.0 %all-gather.3.cloned.1.call-done = bf16[3840,1024]{1,0:T(8,128)(2,1)} async-done(((bf16[480,1024]{1,0:T(8,128)(2,1)}), bf16[3840,1024]{1,0:T(8,128)(2,1)}) %all-gather.3.cloned.1.call-update) | async-done | bytes 7864336 | tf_op jit(solution)/shard_map/all_gather | solution.py:151
  263.3 9.6 %multiply_convert_fusion = bf16[512,1024]{1,0:T(8,128)(2,1)} fusion(bf16[512,3840]{1,0:T(8,128)(2,1)} %collective-permute-done.2, bf16[3840,1024]{1,0:T(8,128)(2,1)} %all-gather.3.cloned.1.call-done), kind=kOutput, calls=%fused_computation.2 | convolution fusion | flops 4027580416 | bytes 12845056 | tf_op jit(solution)/shard_map/dot_general | solution.py:156
  272.9 0.5 collective-permute-start.3
  273.4 0.0 collective-permute-done.7.refs_5_.refs_8_
  273.4 6.6 %collective-permute-start.8 = (bf16[512,2048]{1,0:T(8,128)(2,1)}, bf16[512,2048]{1,0:T(8,128)(2,1)}, u32[]{:S(2)}, u32[]{:S(2)}) collective-permute-start(bf16[512,2048]{1,0:T(8,128)(2,1)} %collective-permute-done.7.refs_5_.refs_8_), channel_id=1, source_target_pairs={{0,2},{2,4},{4,6},{6,8},{8,10},{10,12},{12,14},{14,16},{16,18},{18... | collective-permute-start | bytes 6291464 | tf_op jit(solution)/shard_map/ppermute | solution.py:19
  280.0 0.0 copy-start
  280.0 0.0 copy-start.1
  280.0 0.0 collective-permute-done.3
  280.0 8.8 %broadcast_select_fusion.3 = (bf16[512,1024]{1,0:T(8,128)(2,1)S(1)}, bf16[512,1024]{1,0:T(8,128)(2,1)S(1)}) fusion(bf16[512,1024]{1,0:T(8,128)(2,1)S(1)} %collective-permute-done.3, pred[]{:T(512)S(6)} %eq.2, bf16[512,3840]{1,0:T(8,128)(2,1)} %copy-done.2, bf16[3840,1024]{1,0:T(8,128)(2,1)} %all-gather.3.cloned.1.call-done), kind=kOutput, calls=%fused_computation.14 | convolution fusion | flops 4028628992 | bytes 14942209 | tf_op jit(solution)/shard_map/dot_general | solution.py:155
  288.8 14.3 %collective-permute-done.8.refs_4_.refs_7_ = bf16[512,2048]{1,0:T(8,128)(2,1)} collective-permute-done((bf16[512,2048]{1,0:T(8,128)(2,1)}, bf16[512,2048]{1,0:T(8,128)(2,1)}, u32[]{:S(2)}, u32[]{:S(2)}) %collective-permute-start.8) | collective-permute-done | bytes 2097184 | tf_op jit(solution)/shard_map/ppermute | solution.py:19
  303.0 13.3 %shard_map.78 = (bf16[512,1024]{1,0:T(8,128)(2,1)S(1)}, bf16[512,512]{1,0:T(8,128)(2,1)S(1)}, bf16[512,512]{1,0:T(8,128)(2,1)S(1)}, f32[512,512]{1,0:T(8,128)S(1)}) custom-call(s32[1]{0:T(128)} %bitcast.refs_0_, s32[8]{0:T(128)S(1)} %copy-done.1, bf16[512,1024]{1,0:T(8,128)(2,1)S(1)} %get-tuple-element.21.refs_2_, bf16[512,2048]{1,0:T(8,128)(2,1)S(1)} %copy-done, ...), custom_call_target="tpu_custom_call" | custom-call | flops 6710886400 | bytes 11010048 | tf_op jit(solution)/shard_map/pallas_call | solution.py:93
  316.4 1.9 collective-permute-start.11
  318.3 13.3 %shard_map.77 = (bf16[512,1024]{1,0:T(8,128)(2,1)S(1)}, bf16[512,512]{1,0:T(8,128)(2,1)S(1)}, bf16[512,512]{1,0:T(8,128)(2,1)S(1)}, f32[512,512]{1,0:T(8,128)S(1)}) custom-call(s32[1]{0:T(128)} %bitcast.refs_0_, s32[8]{0:T(128)S(1)} %copy-done.1, bf16[512,1024]{1,0:T(8,128)(2,1)S(1)} %get-tuple-element.20.refs_2_, bf16[512,2048]{1,0:T(8,128)(2,1)S(1)} %copy-done, ...), custom_call_target="tpu_custom_call" | custom-call | flops 6710886400 | bytes 11010048 | tf_op jit(solution)/shard_map/pallas_call | solution.py:93
  331.7 1.9 collective-permute-start.9
  333.6 0.0 collective-permute-done.11
  333.6 0.1 add_convert_fusion.1
  333.7 3.6 collective-permute-start.12
  337.4 6.5 %collective-permute-done.9 = bf16[512,512]{1,0:T(8,128)(2,1)S(1)} collective-permute-done((bf16[512,512]{1,0:T(8,128)(2,1)S(1)}, bf16[512,512]{1,0:T(8,128)(2,1)S(1)}, u32[]{:S(2)}, u32[]{:S(2)}) %collective-permute-start.9) | collective-permute-done | bytes 524320 | tf_op jit(solution)/shard_map/ppermute | solution.py:19
  343.8 0.1 add_convert_fusion.3
  343.9 1.9 collective-permute-start.10
  345.9 1.5 pad_maximum_fusion.1
  347.4 2.0 collective-permute-done.12
  349.4 0.2 add_convert_fusion
  349.6 5.7 %collective-permute-done.10 = bf16[512,512]{1,0:T(8,128)(2,1)S(1)} collective-permute-done((bf16[512,512]{1,0:T(8,128)(2,1)S(1)}, bf16[512,512]{1,0:T(8,128)(2,1)S(1)}, u32[]{:S(2)}, u32[]{:S(2)}) %collective-permute-start.10) | collective-permute-done | bytes 524320 | tf_op jit(solution)/shard_map/ppermute | solution.py:19
  355.3 0.2 add_convert_fusion.2
  355.5 1.1 pad_maximum_fusion.2
  (8 shorter events, 0.0 us)
Async XLA Ops:
  7.2 7.0 %copy-start.5 = (bf16[512,1920]{1,0:T(8,128)(2,1)S(1)}, bf16[512,1920]{1,0:T(8,128)(2,1)}, u32[]{:S(2)}) copy-start(bf16[512,1920]{1,0:T(8,128)(2,1)} %param.6) | copy-start | bytes 5898244
  7.2 8.3 %copy-start.4 = (bf16[240,2048]{1,0:T(8,128)(2,1)S(1)}, bf16[240,2048]{1,0:T(8,128)(2,1)}, u32[]{:S(2)}) copy-start(bf16[240,2048]{1,0:T(8,128)(2,1)} %param.7) | copy-start | bytes 2949124
  7.2 123.0 %all-gather.5.cloned.1.call-start = ((), (), s32[]{:S(2)}) async-start(), calls=%async_computation.1 | async-start | bytes 8847360 | tf_op jit(solution)/shard_map/all_gather | solution.py:149
  8.5 1.9 collective-permute-start.5
  10.3 1.6 collective-permute-start.4
  14.1 249.2 %all-gather.3.cloned.1.call-start = ((), (), s32[]{:S(2)}) async-start(), calls=%async_computation | async-start | bytes 8847360 | tf_op jit(solution)/shard_map/all_gather | solution.py:151
  14.2 44.5 %collective-permute-start = (bf16[512,1920]{1,0:T(8,128)(2,1)S(1)}, bf16[512,1920]{1,0:T(8,128)(2,1)}, u32[]{:S(2)}, u32[]{:S(2)}) collective-permute-start(bf16[512,1920]{1,0:T(8,128)(2,1)S(1)} %copy-done.5), channel_id=1, source_target_pairs={{0,1},{1,0},{2,3},{3,2},{4,5},{5,4},{6,7},{7,6},{8,9},{9,8},{10,11... | collective-permute-start | bytes 5898248 | tf_op jit(solution)/shard_map/ppermute | solution.py:130
  16.3 2.1 collective-permute-start.1
  60.4 1.9 copy-start.2
  65.3 7.8 %collective-permute-start.2 = (bf16[512,3840]{1,0:T(8,128)(2,1)}, bf16[512,3840]{1,0:T(8,128)(2,1)}, u32[]{:S(2)}, u32[]{:S(2)}) collective-permute-start(bf16[512,3840]{1,0:T(8,128)(2,1)} %copy-done.2), channel_id=1, source_target_pairs={{0,2},{2,0},{1,3},{3,1},{4,6},{6,4},{5,7},{7,5},{8,10},{10,8},{9,1... | collective-permute-start | bytes 11796488 | tf_op jit(solution)/shard_map/ppermute | solution.py:116
  130.2 12.0 %copy-start.3 = (bf16[512,3840]{1,0:T(8,128)(2,1)S(1)}, bf16[512,3840]{1,0:T(8,128)(2,1)}, u32[]{:S(2)}) copy-start(bf16[512,3840]{1,0:T(8,128)(2,1)} %copy-done.2) | copy-start | bytes 11796484
  130.2 12.0 %copy-start.6 = (bf16[3840,1024]{1,0:T(8,128)(2,1)S(1)}, bf16[3840,1024]{1,0:T(8,128)(2,1)}, u32[]{:S(2)}) copy-start(bf16[3840,1024]{1,0:T(8,128)(2,1)} %all-gather.5.cloned.1.call-done) | copy-start | bytes 23592964
  139.0 3.3 collective-permute-start.6
  146.9 126.4 %collective-permute-start.7 = (bf16[512,2048]{1,0:T(8,128)(2,1)S(1)}, bf16[512,2048]{1,0:T(8,128)(2,1)}, u32[]{:S(2)}, u32[]{:S(2)}) collective-permute-start(bf16[512,2048]{1,0:T(8,128)(2,1)S(1)} %pad_maximum_fusion.refs_6_.refs_9_), channel_id=1, source_target_pairs={{0,2},{2,4},{4,6},{6,8},{8,10},{10,12},{12,14},{14,16},{16,18},{18... | collective-permute-start | bytes 6291464 | tf_op jit(solution)/shard_map/ppermute | solution.py:19
  272.9 7.1 %collective-permute-start.3 = (bf16[512,1024]{1,0:T(8,128)(2,1)}, bf16[512,1024]{1,0:T(8,128)(2,1)S(1)}, u32[]{:S(2)}, u32[]{:S(2)}) collective-permute-start(bf16[512,1024]{1,0:T(8,128)(2,1)} %multiply_convert_fusion), channel_id=1, source_target_pairs={{0,2},{2,0},{1,3},{3,1},{4,6},{6,4},{5,7},{7,5},{8,10},{10,8},{9,1... | collective-permute-start | bytes 3145736 | tf_op jit(solution)/shard_map/ppermute | solution.py:116
  273.4 29.7 %collective-permute-start.8 = (bf16[512,2048]{1,0:T(8,128)(2,1)}, bf16[512,2048]{1,0:T(8,128)(2,1)}, u32[]{:S(2)}, u32[]{:S(2)}) collective-permute-start(bf16[512,2048]{1,0:T(8,128)(2,1)} %collective-permute-done.7.refs_5_.refs_8_), channel_id=1, source_target_pairs={{0,2},{2,4},{4,6},{6,8},{8,10},{10,12},{12,14},{14,16},{16,18},{18... | collective-permute-start | bytes 6291464 | tf_op jit(solution)/shard_map/ppermute | solution.py:19
  280.0 23.1 %copy-start = (bf16[512,2048]{1,0:T(8,128)(2,1)S(1)}, bf16[512,2048]{1,0:T(8,128)(2,1)}, u32[]{:S(2)}) copy-start(bf16[512,2048]{1,0:T(8,128)(2,1)} %refs_3_.3) | copy-start | bytes 6291460
  280.0 23.1 %copy-start.1 = (s32[8]{0:T(128)S(1)}, s32[8]{0:T(128)}, u32[]{:S(2)}) copy-start(s32[8]{0:T(128)} %refs_1_.3) | copy-start | bytes 100
  316.4 17.2 %collective-permute-start.11 = (bf16[512,512]{1,0:T(8,128)(2,1)S(1)}, bf16[512,512]{1,0:T(8,128)(2,1)S(1)}, u32[]{:S(2)}, u32[]{:S(2)}) collective-permute-start(bf16[512,512]{1,0:T(8,128)(2,1)S(1)} %get-tuple-element.15), channel_id=1, source_target_pairs={{2,0},{4,2},{6,4},{8,6},{10,8},{12,10},{14,12},{16,14},{18,16},{20... | collective-permute-start | bytes 1572872 | tf_op jit(solution)/shard_map/ppermute | solution.py:19
  331.7 12.2 %collective-permute-start.9 = (bf16[512,512]{1,0:T(8,128)(2,1)S(1)}, bf16[512,512]{1,0:T(8,128)(2,1)S(1)}, u32[]{:S(2)}, u32[]{:S(2)}) collective-permute-start(bf16[512,512]{1,0:T(8,128)(2,1)S(1)} %get-tuple-element.12), channel_id=1, source_target_pairs={{2,0},{4,2},{6,4},{8,6},{10,8},{12,10},{14,12},{16,14},{18,16},{20... | collective-permute-start | bytes 1572872 | tf_op jit(solution)/shard_map/ppermute | solution.py:19
  333.7 15.7 %collective-permute-start.12 = (bf16[512,512]{1,0:T(8,128)(2,1)S(1)}, bf16[512,512]{1,0:T(8,128)(2,1)S(1)}, u32[]{:S(2)}, u32[]{:S(2)}) collective-permute-start(bf16[512,512]{1,0:T(8,128)(2,1)S(1)} %add_convert_fusion.1), channel_id=1, source_target_pairs={{2,0},{4,2},{6,4},{8,6},{10,8},{12,10},{14,12},{16,14},{18,16},{20... | collective-permute-start | bytes 1572872 | tf_op jit(solution)/shard_map/ppermute | solution.py:19
  343.9 11.4 %collective-permute-start.10 = (bf16[512,512]{1,0:T(8,128)(2,1)S(1)}, bf16[512,512]{1,0:T(8,128)(2,1)S(1)}, u32[]{:S(2)}, u32[]{:S(2)}) collective-permute-start(bf16[512,512]{1,0:T(8,128)(2,1)S(1)} %add_convert_fusion.3), channel_id=1, source_target_pairs={{2,0},{4,2},{6,4},{8,6},{10,8},{12,10},{14,12},{16,14},{18,16},{20... | collective-permute-start | bytes 1572872 | tf_op jit(solution)/shard_map/ppermute | solution.py:19
Sparse Core Ops, SparseCore 0:
  14.2 115.9 all-gather.4
  133.0 130.2 all-gather.2
